TPU v7x, 256 devices: a whole 4x4x8 slice. The times are simulated.
256 devices in a mesh: loop: 4 (over y_hi, core), inner: 64 (over z, x, y_lo).
Axes of the slice: x: 4, y: 4 (y_hi: 2, y_lo: 2; y = y_hi * 2 + y_lo), z: 8, core: 2. Of those that a mesh axis runs over, the one named last changes fastest.
Arguments:
- snapshots: bfloat16 [65536, 1024], P(('loop', 'inner')), may hold values from -6 to 6
- bins: int32 [65536], replicated, may hold values from 0 to 511, as said below
- pairs: int32 [2048, 2], replicated, may hold values from 0 to 511, as said below
- start_weights: bfloat16 [1024, 32], replicated, may hold values from -0.1875 to 0.1875
Outputs:
- basis: float32 [65536, 96], P(('loop', 'inner'))
- coefficients: float32 [4, 32, 32], replicated
Inputs may be any that keep to these rules, and one draw needn't show every extreme that they name: `bins`: the snapshot in row n has a bin in [r * 8, (r + 1) * 8), where r = (n // 256) mod (64). `pairs`: every row (a, b) has a <= b <= a + 8; every bin is paired with itself.
All inputs are finite; a program needn't handle non-finite values.
Results may differ from a plain program's by a relative error of at most 0.0003.
Values may be sent and summed in bfloat16 or wider, within the bound.
A program may use at most 64 MiB of HBM per device.

v0:
```python
import jax
import jax.numpy as jnp
from jax import lax
from jax.sharding import PartitionSpec as P

STEPS = 2
BINS_COL = 8


def extended(cells, sides, width):
    for axis, dim in sides:
        count = lax.axis_size(axis)
        ends = count - 1
        head = lax.slice_in_dim(cells, 0, width, axis=dim)
        tail = lax.slice_in_dim(cells, cells.shape[dim] - width, cells.shape[dim], axis=dim)
        cells = jnp.concatenate(
            [
                lax.ppermute(tail, axis, [(i, (i + 1) % count) for i in range(ends)]),
                cells,
                lax.ppermute(head, axis, [((i + 1) % count, i) for i in range(ends)]),
            ],
            axis=dim,
        )
    return cells


def matches(values, targets):
    return (values[:, None] == targets[None, :]).astype(jnp.float32)


def local_gram(left, right):
    return jnp.dot(left.T, right, precision=lax.Precision.HIGHEST)


def finish(matrix, gram_total):
    lower_factor = jnp.linalg.cholesky(gram_total)
    result = lax.linalg.triangular_solve(
        lower_factor, matrix, left_side=False, lower=True, transpose_a=True
    )
    return (result, lower_factor.T)


def local(snapshots, bins, pairs, start_weights):
    row_count, features = snapshots.shape
    block_width = start_weights.shape[1]
    n_loop = lax.axis_size("loop")
    n_inner = lax.axis_size("inner")
    column = lax.axis_index("inner")
    group = lax.axis_index("loop")
    bin_grid = jnp.pad(
        bins.reshape(n_loop, n_inner, row_count), ((0, 0), (1, 1), (0, 0)), constant_values=-1
    )
    stacked = lax.all_gather(snapshots[None], "loop", axis=0, tiled=True)
    partner_rows = extended(stacked, (("inner", 1),), row_count)
    tile_rows = partner_rows.reshape(n_loop * 3 * row_count, features)
    tile_bins = lax.dynamic_slice_in_dim(bin_grid, column, 3, 1).reshape(-1)
    my_bins = lax.dynamic_slice_in_dim(bins, (group * n_inner + column) * row_count, row_count)
    bin_base = column * BINS_COL
    my_ids = bin_base + jnp.arange(BINS_COL, dtype=jnp.int32)
    window_ids = bin_base - BINS_COL + jnp.arange(3 * BINS_COL, dtype=jnp.int32)
    left_bins = pairs[:, 0]
    right_bins = pairs[:, 1]
    pair_count = jnp.dot(
        matches(left_bins, my_ids).T,
        matches(right_bins, window_ids),
        precision=lax.Precision.HIGHEST,
    )
    pair_count = pair_count + jnp.dot(
        matches(right_bins, my_ids).T,
        matches(left_bins, window_ids),
        precision=lax.Precision.HIGHEST,
    )
    linked_bins = jnp.where(pair_count > 0.5, 1.0, 0.0).astype(jnp.float32)
    my_hot = matches(my_bins, my_ids)
    row_links = jnp.dot(my_hot, linked_bins)
    mine_wide = snapshots.astype(jnp.float32)
    mine_norms = jnp.sum(mine_wide * mine_wide, axis=1)
    epsilon = features / 3.0
    part_hot = matches(tile_bins, window_ids) * (tile_bins >= 0).astype(jnp.float32)[:, None]
    band_mask = jnp.dot(row_links, part_hot.T)
    part_wide = tile_rows.astype(jnp.float32)
    part_norms = jnp.sum(part_wide * part_wide, axis=1)
    products = lax.dot_general(
        snapshots, tile_rows, (((1,), (1,)), ((), ())), preferred_element_type=jnp.float32
    )
    distance = mine_norms[:, None] + part_norms[None, :] - 2.0 * products
    kept_tiles = [band_mask * jnp.exp(-distance / epsilon)]

    def current_kernel(which):
        return kept_tiles[which]

    degree = jnp.sum(current_kernel(0), axis=1)
    inv_root = lax.rsqrt(degree)
    start_block = jnp.dot(snapshots, start_weights, preferred_element_type=jnp.float32)
    start_total = lax.psum(local_gram(start_block, start_block), ("loop", "inner"))
    current, unused = finish(start_block, start_total)
    basis_blocks = [current]
    coefficients = []
    previous = current
    prev_b = jnp.zeros((block_width, block_width), jnp.float32)
    for lanczos_step in range(STEPS):
        scaled = inv_root[:, None] * current
        vec_stack = lax.all_gather(scaled[None], "loop", axis=0, tiled=True)
        vec_strip = extended(vec_stack, (("inner", 1),), row_count)
        strip = vec_strip.reshape(n_loop * 3 * row_count, block_width)
        total = jnp.dot(current_kernel(0), strip, precision=lax.Precision.HIGHEST)
        image = inv_root[:, None] * total
        projected = lax.psum(local_gram(current, image), ("loop", "inner"))
        image = image - jnp.dot(current, projected, precision=lax.Precision.HIGHEST)
        if lanczos_step > 0:
            image = image - jnp.dot(previous, prev_b.T, precision=lax.Precision.HIGHEST)
        gram_total = lax.psum(local_gram(image, image), ("loop", "inner"))
        following, factor = finish(image, gram_total)
        coefficients.append(projected)
        coefficients.append(factor)
        previous = current
        prev_b = factor
        current = following
        basis_blocks.append(current)
    return (jnp.concatenate(basis_blocks, axis=1), jnp.stack(coefficients))


def solution(mesh):
    in_specs = (P(("loop", "inner"), None), P(), P(), P())
    out_specs = (P(("loop", "inner"), None), P())
    return jax.shard_map(local, mesh=mesh, in_specs=in_specs, out_specs=out_specs, check_vma=False)
```

profile of v0, /device:TPU:1, one launch (start us, length us, event | category | flops | bytes accessed | tf_op | source)
XLA Modules:
  0.0 579.3 jit_solution(10393950573843033094)
XLA Ops:
  9.8 1.3 fusion.49
  11.2 90.2 %psum.35 = f32[32,32]{0,1:T(8,128)S(1)} all-reduce(f32[32,32]{0,1:T(8,128)S(1)} %fusion.50), channel_id=1, replica_groups=mesh['loop'=4,'inner'=64] {'loop','inner'}, use_global_device_ids=true, to_apply=%region_0.1 | all-reduce | flops 1024 | bytes 8192 | tf_op jit(solution)/shard_map/psum | solution.py:95
  101.5 1.3 collective-permute-start.1
  102.8 5.3 collective-permute-start
  108.1 2.9 cholesky.59
  112.4 2.4 custom-call.7
  114.8 1.2 multiply_reduce_fusion.1
  118.8 31.0 %collective-permute-done.1 = bf16[4,256,1024]{2,1,0:T(8,128)(2,1)S(1)} collective-permute-done((bf16[4,256,1024]{2,1,0:T(8,128)(2,1)}, bf16[4,256,1024]{2,1,0:T(8,128)(2,1)S(1)}, u32[]{:S(2)}, u32[]{:S(2)}) %collective-permute-start.1) | collective-permute-done | bytes 2097184 | tf_op jit(solution)/shard_map/ppermute | solution.py:20
  149.8 44.7 %collective-permute-done = bf16[4,256,1024]{2,1,0:T(8,128)(2,1)} collective-permute-done((bf16[4,256,1024]{2,1,0:T(8,128)(2,1)}, bf16[4,256,1024]{2,1,0:T(8,128)(2,1)}, u32[]{:S(2)}, u32[]{:S(2)}) %collective-permute-start) | collective-permute-done | bytes 2097184 | tf_op jit(solution)/shard_map/ppermute | solution.py:18
  194.5 3.6 multiply_reduce_fusion
  198.2 3.5 fusion
  201.7 3.1 fusion.46
  205.0 7.2 %all-gather.1 = f32[1024,32]{0,1:T(8,128)S(1)} all-gather(f32[256,32]{0,1:T(8,128)S(1)} %get-tuple-element.20), channel_id=3, replica_groups=mesh['loop'=4,'inner'=64] {'loop'}, dimensions={0}, use_global_device_ids=true | all-gather | bytes 163840 | tf_op jit(solution)/shard_map/all_gather | solution.py:103
  212.3 1.3 collective-permute-start.3
  213.6 4.8 collective-permute-start.2
  218.4 1.9 collective-permute-done.3
  220.2 3.2 collective-permute-done.2
  223.6 2.8 convolution_multiply_fusion.3
  226.5 80.3 %psum.36 = f32[32,32]{0,1:T(8,128)S(1)} all-reduce(f32[32,32]{0,1:T(8,128)S(1)} %fusion.51), channel_id=1, replica_groups=mesh['loop'=4,'inner'=64] {'loop','inner'}, use_global_device_ids=true, to_apply=%region_6.9 | all-reduce | flops 1024 | bytes 8192 | tf_op jit(solution)/shard_map/psum | solution.py:108
  307.2 75.5 %psum.37 = f32[32,32]{0,1:T(8,128)S(1)} all-reduce(f32[32,32]{0,1:T(8,128)S(1)} %fusion.52), channel_id=1, replica_groups=mesh['loop'=4,'inner'=64] {'loop','inner'}, use_global_device_ids=true, to_apply=%region_7.10 | all-reduce | flops 1024 | bytes 8192 | tf_op jit(solution)/shard_map/psum | solution.py:112
  382.8 2.9 cholesky.70
  387.6 2.4 custom-call.8
  390.3 7.4 %all-gather.2 = f32[1024,32]{0,1:T(8,128)S(1)} all-gather(f32[256,32]{0,1:T(8,128)S(1)} %get-tuple-element.22), channel_id=4, replica_groups=mesh['loop'=4,'inner'=64] {'loop'}, dimensions={0}, use_global_device_ids=true | all-gather | bytes 163840 | tf_op jit(solution)/shard_map/all_gather | solution.py:103
  397.8 1.3 collective-permute-start.5
  399.1 4.0 collective-permute-start.4
  403.1 1.5 collective-permute-done.5
  404.7 2.6 collective-permute-done.4
  407.5 3.5 convolution_multiply_fusion.2
  411.1 76.5 %psum.38 = f32[32,32]{0,1:T(8,128)S(1)} all-reduce(f32[32,32]{0,1:T(8,128)S(1)} %fusion.53), channel_id=1, replica_groups=mesh['loop'=4,'inner'=64] {'loop','inner'}, use_global_device_ids=true, to_apply=%region_8.11 | all-reduce | flops 1024 | bytes 8192 | tf_op jit(solution)/shard_map/psum | solution.py:108
  488.7 75.3 %psum.39 = f32[32,32]{0,1:T(8,128)S(1)} all-reduce(f32[32,32]{0,1:T(8,128)S(1)} %fusion.54), channel_id=1, replica_groups=mesh['loop'=4,'inner'=64] {'loop','inner'}, use_global_device_ids=true, to_apply=%region_9.12 | all-reduce | flops 1024 | bytes 8192 | tf_op jit(solution)/shard_map/psum | solution.py:112
  564.1 2.9 cholesky.81
  568.4 2.4 custom-call.9
  (62 shorter events, 14.6 us)
Async XLA Ops:
  7.2 2.6 copy-start
  7.2 94.4 %all-gather.5.cloned.1.call-start = ((), (), s32[]{:S(2)}) async-start(), calls=%async_computation | async-start | bytes 2621440 | tf_op jit(solution)/shard_map/all_gather | solution.py:53
  101.5 48.3 %collective-permute-start.1 = (bf16[4,256,1024]{2,1,0:T(8,128)(2,1)}, bf16[4,256,1024]{2,1,0:T(8,128)(2,1)S(1)}, u32[]{:S(2)}, u32[]{:S(2)}) collective-permute-start(bf16[4,256,1024]{2,1,0:T(8,128)(2,1)} %bitcast.93), channel_id=1, source_target_pairs={{1,0},{2,1},{3,2},{4,3},{5,4},{6,5},{7,6},{8,7},{9,8},{10,9},{11,1... | collective-permute-start | bytes 6291464 | tf_op jit(solution)/shard_map/ppermute | solution.py:20
  102.8 91.7 %collective-permute-start = (bf16[4,256,1024]{2,1,0:T(8,128)(2,1)}, bf16[4,256,1024]{2,1,0:T(8,128)(2,1)}, u32[]{:S(2)}, u32[]{:S(2)}) collective-permute-start(bf16[4,256,1024]{2,1,0:T(8,128)(2,1)} %bitcast.94), channel_id=1, source_target_pairs={{0,1},{1,2},{2,3},{3,4},{4,5},{5,6},{6,7},{7,8},{8,9},{9,10},{10,1... | collective-permute-start | bytes 6291464 | tf_op jit(solution)/shard_map/ppermute | solution.py:18
  118.8 79.3 %copy-start.1 = (bf16[256,1024]{1,0:T(8,128)(2,1)S(1)}, bf16[256,1024]{1,0:T(8,128)(2,1)}, u32[]{:S(2)}) copy-start(bf16[256,1024]{1,0:T(8,128)(2,1)} %param.7) | copy-start | bytes 1572868
  204.8 185.5 %copy-start.5 = (f32[256]{0:T(256)}, f32[256]{0:T(256)S(1)}, u32[]{:S(2)}) copy-start(f32[256]{0:T(256)S(1)} %rsqrt.7) | copy-start | bytes 3076
  212.3 7.9 %collective-permute-start.3 = (f32[4,256,32]{1,0,2:T(4,128)S(1)}, f32[4,256,32]{1,0,2:T(4,128)S(1)}, u32[]{:S(2)}, u32[]{:S(2)}) collective-permute-start(f32[4,256,32]{1,0,2:T(4,128)S(1)} %reshape.60), channel_id=1, source_target_pairs={{1,0},{2,1},{3,2},{4,3},{5,4},{6,5},{7,6},{8,7},{9,8},{10,9},{11,1... | collective-permute-start | bytes 393224 | tf_op jit(solution)/shard_map/ppermute | solution.py:20
  213.6 9.8 %collective-permute-start.2 = (f32[4,256,32]{1,0,2:T(4,128)S(1)}, f32[4,256,32]{1,0,2:T(4,128)S(1)}, u32[]{:S(2)}, u32[]{:S(2)}) collective-permute-start(f32[4,256,32]{1,0,2:T(4,128)S(1)} %reshape.60), channel_id=1, source_target_pairs={{0,1},{1,2},{2,3},{3,4},{4,5},{5,6},{6,7},{7,8},{8,9},{9,10},{10,1... | collective-permute-start | bytes 393224 | tf_op jit(solution)/shard_map/ppermute | solution.py:18
  306.9 83.4 %copy-start.2 = (f32[32,32]{0,1:T(8,128)}, f32[32,32]{0,1:T(8,128)S(1)}, u32[]{:S(2)}) copy-start(f32[32,32]{0,1:T(8,128)S(1)} %psum.36) | copy-start | bytes 12292
  397.8 173.9 %copy-start.3 = (f32[32,32]{0,1:T(8,128)S(1)}, f32[32,32]{0,1:T(8,128)}, u32[]{:S(2)}) copy-start(f32[32,32]{0,1:T(8,128)} %copy-done.2) | copy-start | bytes 12292
  397.8 173.9 %copy-start.4 = (f32[1,32,32]{1,2,0:T(8,128)S(1)}, f32[1,32,32]{1,2,0:T(8,128)}, u32[]{:S(2)}) copy-start(f32[1,32,32]{1,2,0:T(8,128)} %get-tuple-element.12) | copy-start | bytes 12292
  397.8 6.8 %collective-permute-start.5 = (f32[4,256,32]{1,0,2:T(4,128)S(1)}, f32[4,256,32]{1,0,2:T(4,128)S(1)}, u32[]{:S(2)}, u32[]{:S(2)}) collective-permute-start(f32[4,256,32]{1,0,2:T(4,128)S(1)} %reshape.61), channel_id=1, source_target_pairs={{1,0},{2,1},{3,2},{4,3},{5,4},{6,5},{7,6},{8,7},{9,8},{10,9},{11,1... | collective-permute-start | bytes 393224 | tf_op jit(solution)/shard_map/ppermute | solution.py:20
  399.1 8.2 %collective-permute-start.4 = (f32[4,256,32]{1,0,2:T(4,128)S(1)}, f32[4,256,32]{1,0,2:T(4,128)S(1)}, u32[]{:S(2)}, u32[]{:S(2)}) collective-permute-start(f32[4,256,32]{1,0,2:T(4,128)S(1)} %reshape.61), channel_id=1, source_target_pairs={{0,1},{1,2},{2,3},{3,4},{4,5},{5,6},{6,7},{7,8},{8,9},{9,10},{10,1... | collective-permute-start | bytes 393224 | tf_op jit(solution)/shard_map/ppermute | solution.py:18
Sparse Core Ops, SparseCore 0:
  9.8 33.8 all-gather.4
where the time goes:
time: 581 us; the launch traced here: 579 us
  blocking collectives  413 us (71%)
  waiting for transfers between devices  85.5 us (15%)
  other arithmetic  26.3 us (5%)
  matrix products  18.7 us (3%)
  starting transfers between devices  17.9 us (3%)
  between operations  14.3 us (2%)
    psum x2, blocking collectives, local(): projected = lax.psum(local_gram(current, image), ('loop', 'inner'))  157 us
    psum x2, blocking collectives, local(): gram_total = lax.psum(local_gram(image, image), ('loop', 'inner'))  151 us
    psum x1, blocking collectives, local(): lax.psum(local_gram(start_block, start_block), ('loop', 'inner'))  90.2 us
    ppermute x3, waiting for transfers between devices, extended(): lax.ppermute(tail, axis, [(i, (i + 1) % count) for i in range(ends)])  50.5 us
    ppermute x3, waiting for transfers between devices, extended(): lax.ppermute(head, axis, [((i + 1) % count, i) for i in range(ends)])  34.4 us
    all_gather x2, blocking collectives, local(): vec_stack = lax.all_gather(scaled[None], 'loop', axis=0, tiled=True)  14.7 us
    ppermute x3, starting transfers between devices, extended(): lax.ppermute(tail, axis, [(i, (i + 1) % count) for i in range(ends)])  14 us
  transfers between devices with their start and end apart: 7, of which 6 were waited for; matrix products, arithmetic and copies ran while one was open for 2% of the time, Pallas kernels for 0%

commit v1 on v0

v1 whole, which is shorter than its diff:
```python
import functools

import jax
import jax.numpy as jnp
from jax import lax
from jax.experimental import pallas as pl
from jax.experimental.pallas import tpu as pltpu
from jax.sharding import PartitionSpec as P

MESH = pl.DeviceIdType.MESH
HIGHEST = lax.Precision.HIGHEST
F32 = jnp.float32
BF16 = jnp.bfloat16

NX, NY, NZ = 4, 4, 8
BINS_COL = 8
WINDOW = 32
ROWS = 256
BLOCK = 32
PARTNERS = 12
CHUNKS = 4
CHUNK = ROWS // CHUNKS
DIRECT = 1
HALF = ROWS // 2


def mm(a, b):
    return lax.dot_general(a, b, (((1,), (0,)), ((), ())), precision=HIGHEST, preferred_element_type=F32)


def mm_t(a, b):
    return lax.dot_general(a, b, (((1,), (1,)), ((), ())), precision=HIGHEST, preferred_element_type=F32)


def t_mm(a, b):
    return mm(a.T, b)


def split(v):
    high = v.astype(BF16)
    return high, (v - high.astype(F32)).astype(BF16)


def pack(m):
    return jnp.concatenate([m[8 * g : 8 * g + 8, :] for g in range(4)], axis=1)


def unpack(p):
    return jnp.concatenate([p[:, 32 * g : 32 * g + 32] for g in range(4)], axis=0)


def factorise(gram):
    sub = lax.broadcasted_iota(jnp.int32, (BLOCK, BLOCK), 0)
    lane = lax.broadcasted_iota(jnp.int32, (BLOCK, BLOCK), 1)
    eye = (sub == lane).astype(F32)
    work = jnp.concatenate([gram, eye], axis=1)
    below = lax.broadcasted_iota(jnp.int32, (BLOCK, 2 * BLOCK), 0)
    scale = jnp.zeros((BLOCK, 2 * BLOCK), F32)
    for k in range(BLOCK):
        row = jnp.broadcast_to(work[k : k + 1, :], (BLOCK, 2 * BLOCK))
        column = jnp.broadcast_to(work[:, k : k + 1], (BLOCK, 2 * BLOCK))
        pivot = jnp.broadcast_to(column[k : k + 1, :], (BLOCK, 2 * BLOCK))
        scale = jnp.where(below == k, pivot, scale)
        work = work - jnp.where(below > k, column / pivot, 0.0) * row
    work = work * lax.rsqrt(scale)
    upper = jnp.where(lane >= sub, work[:, :BLOCK], 0.0)
    return upper, work[:, BLOCK:]


def kernel(
    x_ref, bins_ref, pairs_ref, wt_ref, out_ref, coef_ref,
    xb, kh, kl, hot, links, st, sq_row, deg, irb, zb, vb, core_buf, plane_buf, line_buf,
    x_send, x_first, x_fwd, x_core, ir_sem, v_sem, ar_sem,
):
    features = x_ref.shape[1]
    group = lax.axis_index("loop")
    inner = lax.axis_index("inner")
    core = group % 2
    odd = inner % 2
    y = (group // 2) * 2 + odd
    x = (inner // 2) % NX
    z = inner // (2 * NX)

    def device(c, xx, yy, zz):
        yy = yy % NY
        return ((yy // 2) * 2 + c, (zz % NZ) * (2 * NX) + (xx % NX) * 2 + yy % 2)

    def near(dc, dy, di):
        yy = (y + dy) % NY
        return ((yy // 2) * 2 + (core + dc) % 2, ((inner // 2 + di) % (NX * NZ)) * 2 + yy % 2)

    step = 1 - 2 * odd
    other = near(1, 0, 0)

    barrier = pltpu.get_barrier_semaphore()
    greeted = [other]
    greeted += [device(core, x + a, y + b, z) for a in range(NX) for b in range(NY) if a or b]
    greeted += [device(core, x, y, z + a) for a in range(1, NZ)]
    greeted += [near(1, dy, 0) for dy in (1, 2, 3)]
    greeted += [near(dc, dy, -step) for dc in (0, 1) for dy in (1, 3)]
    greeted += [near(0, 0, 1), near(0, 0, -1)]
    for d in greeted:
        pl.semaphore_signal(barrier, inc=1, device_id=d, device_id_type=MESH)
    pl.semaphore_wait(barrier, len(greeted))

    def remote(src, dst, send, recv, target):
        return pltpu.make_async_remote_copy(
            src_ref=src, dst_ref=dst, send_sem=send, recv_sem=recv, device_id=target, device_id_type=MESH
        )

    def rows_of(chunk):
        return pl.ds(chunk * CHUNK, CHUNK)

    def push(src, slot, chunk, recv, target):
        source = x_ref.at[rows_of(chunk)] if src is None else xb.at[src, rows_of(chunk)]
        remote(source, xb.at[slot, rows_of(chunk)], x_send, recv, target).start()

    def arrived(ref, sem):
        pltpu.make_async_copy(ref, ref, sem).wait()

    up = list(range(CHUNKS))
    down = up[CHUNKS // 2 :] + up[: CHUNKS // 2]
    far_up, far_down = up[CHUNKS - DIRECT :], down[CHUNKS - DIRECT :]
    for k in range(CHUNKS):
        push(None, 3, up[k], x_first.at[1, up[k]], near(0, 1, 0))
        push(None, 2, down[k], x_first.at[0, down[k]], near(0, -1, 0))
        if k < DIRECT:
            push(None, 6, far_up[k], x_first.at[4, far_up[k]], near(0, 1, -step))
            push(None, 5, far_down[k], x_first.at[3, far_down[k]], near(0, -1, -step))
    remote(x_ref, xb.at[1], x_send, x_core.at[0, 0], other).start()

    def sum_start(n, packed):
        rows = packed.shape[0]
        core_buf[n, 0, pl.ds(0, rows)] = packed
        remote(
            core_buf.at[n, 0, pl.ds(0, rows)], core_buf.at[n, 1, pl.ds(0, rows)],
            ar_sem.at[n, 0], ar_sem.at[n, 1], other,
        ).start()

    def sum_plane(n, rows):
        arrived(core_buf.at[n, 1, pl.ds(0, rows)], ar_sem.at[n, 1])
        both = core_buf[n, 0, pl.ds(0, rows)] + core_buf[n, 1, pl.ds(0, rows)]
        mine = x * NY + y
        plane_buf[n, mine, pl.ds(0, rows)] = both
        place = plane_buf.at[n, mine, pl.ds(0, rows)]

        def send(k, carry):
            remote(
                place, place, ar_sem.at[n, 2], ar_sem.at[n, 3], device(core, x + k // NY, y + k % NY, z)
            ).start()
            return carry

        lax.fori_loop(1, NX * NY, send, 0)

    def sum_line(n, rows):
        span = plane_buf.at[n, pl.ds(0, NX * NY - 1), pl.ds(0, rows)]
        arrived(span, ar_sem.at[n, 3])
        total = jnp.sum(plane_buf[n, :, pl.ds(0, rows)], axis=0)
        line_buf[n, z, pl.ds(0, rows)] = total
        place = line_buf.at[n, z, pl.ds(0, rows)]

        def send(k, carry):
            remote(place, place, ar_sem.at[n, 4], ar_sem.at[n, 5], device(core, x, y, z + k)).start()
            return carry

        lax.fori_loop(1, NZ, send, 0)

    def sum_end(n, rows):
        arrived(line_buf.at[n, pl.ds(0, NZ - 1), pl.ds(0, rows)], ar_sem.at[n, 5])
        return jnp.sum(line_buf[n, :, pl.ds(0, rows)], axis=0)

    def sum_drain(n, rows):
        arrived(core_buf.at[n, 0, pl.ds(0, rows)], ar_sem.at[n, 0])
        arrived(plane_buf.at[n, pl.ds(0, NX * NY - 1), pl.ds(0, rows)], ar_sem.at[n, 2])
        arrived(line_buf.at[n, pl.ds(0, NZ - 1), pl.ds(0, rows)], ar_sem.at[n, 4])

    own = x_ref[...]
    wt = wt_ref[...]
    start = lax.dot_general(wt, own, (((1,), (1,)), ((), ())), preferred_element_type=F32)
    st[:, pl.ds(0, ROWS)] = start
    sum_start(0, pack(mm_t(start, start)))

    pairs = pairs_ref[...]
    left, right = pairs[0:1, :], pairs[1:2, :]
    count = pairs.shape[1]
    my_base = inner * BINS_COL
    window_base = my_base - BINS_COL

    def one_hot(values, base, width):
        ids = lax.broadcasted_iota(jnp.int32, (width, values.shape[1]), 0)
        return jnp.where(values - base == ids, 1.0, 0.0).astype(F32)

    def count_pairs(mine, theirs):
        return lax.dot_general(
            one_hot(mine, my_base, BINS_COL).astype(BF16), one_hot(theirs, window_base, WINDOW).astype(BF16),
            (((1,), (1,)), ((), ())), preferred_element_type=F32,
        )

    linked = jnp.where(count_pairs(left, right) + count_pairs(right, left) > 0.5, 1.0, 0.0)

    def bins_of(block):
        eight = bins_ref[pl.ds(pl.multiple_of((block // 4) * 8, 8), 8), :]
        which = lax.broadcasted_iota(jnp.int32, eight.shape, 0) - 2 * (block % 4)
        first = jnp.sum(jnp.where(which == 0, eight, 0), axis=0, keepdims=True)
        second = jnp.sum(jnp.where(which == 1, eight, 0), axis=0, keepdims=True)
        return jnp.concatenate([first, second], axis=1)

    n_inner = NX * NZ * 2
    my_bins = bins_of(group * n_inner + inner)
    links[...] = mm(linked.T, one_hot(my_bins, my_base, BINS_COL)).astype(BF16)

    def set_hot(slot, where, valid):
        hits = one_hot(bins_of(where[0] * n_inner + where[1]), window_base, WINDOW)
        if valid is not None:
            hits = hits * valid
        hot[slot] = hits.T.astype(BF16)

    across = jnp.where((inner == 0) | (inner == n_inner - 1), 0.0, 1.0).astype(F32)
    set_hot(0, (group, inner), None)
    set_hot(1, other, None)
    for dc in (0, 1):
        for slot, dy in ((2, 1), (3, -1), (4, 2)):
            set_hot(slot + 5 * dc, near(dc, dy, 0), None)
        for slot, dy in ((5, 1), (6, -1)):
            set_hot(slot + 5 * dc, near(dc, dy, -step), across)

    wide = own.astype(F32)
    sq_high, sq_low = split(wide * wide)
    ones = jnp.ones((16, features), BF16)
    norms = lax.dot_general(ones, sq_high, (((1,), (1,)), ((), ())), preferred_element_type=F32)
    norms = norms + lax.dot_general(ones, sq_low, (((1,), (1,)), ((), ())), preferred_element_type=F32)
    sq_row[...] = norms[0:8, :]
    xb[0] = own
    deg[...] = jnp.zeros_like(deg)

    def tile(slot, half):
        span = pl.ds(pl.multiple_of(half * HALF, HALF), HALF)
        theirs = xb[slot, span, :]
        theirs_wide = theirs.astype(F32)
        their_norm = jnp.sum(theirs_wide * theirs_wide, axis=1, keepdims=True)
        products = lax.dot_general(theirs, x_ref[...], (((1,), (1,)), ((), ())), preferred_element_type=F32)
        distance = their_norm + sq_row[0:1, :] - 2.0 * products
        mask = jnp.dot(hot[slot, span, :], links[...], preferred_element_type=F32)
        value = mask * jnp.exp(distance * (-3.0 / features))
        deg[...] += jnp.sum(value.reshape(HALF // 8, 8, ROWS), axis=0)
        high, low = split(value)
        kh[slot, span, :] = high
        kl[slot, span, :] = low

    def whole(slot):
        tile(slot, 0)
        tile(slot, 1)

    def image(slot):
        return lax.dot_general(wt_ref[...], xb[slot], (((1,), (1,)), ((), ())), preferred_element_type=F32)

    def forward(slot, chunk, target_slot, recv, target):
        push(slot, target_slot, chunk, recv, target)

    def got(slot, chunk):
        arrived(xb.at[slot, rows_of(chunk)], x_first.at[slot - 2, chunk])

    def to_core(slot, half):
        span = pl.ds(half * HALF, HALF)
        remote(xb.at[slot, span], xb.at[slot + 5, span], x_send, x_fwd.at[slot - 2, half], other).start()

    def got_core(slot, half):
        arrived(xb.at[slot, pl.ds(half * HALF, HALF)], x_fwd.at[slot - 7, half])

    sum_plane(0, 8)
    whole(0)
    arrived(xb.at[1], x_core.at[0, 0])
    whole(1)

    per = CHUNKS // 2
    for k in range(CHUNKS):
        a, b = down[k], up[k]
        got(2, a)
        if k < CHUNKS - DIRECT:
            push(2, 5, a, x_first.at[3, a], near(0, 0, step))
        if k < per:
            push(2, 4, a, x_first.at[2, a], near(0, -1, 0))
        got(3, b)
        if k < CHUNKS - DIRECT:
            push(3, 6, b, x_first.at[4, b], near(0, 0, step))
        if k < per:
            push(3, 4, b, x_first.at[2, b], near(0, 1, 0))
        if k % per == per - 1:
            to_core(2, a // per)
            to_core(3, b // per)
            tile(2, a // per)
            tile(3, b // per)
    sum_line(0, 8)
    for h in (0, 1):
        for s, halves in ((7, (1, 0)), (8, (0, 1))):
            got_core(s, halves[h])
            tile(s, halves[h])
    for h in (0, 1):
        for chunk in range(per * h, per * h + per):
            got(4, chunk)
        to_core(4, h)
        tile(4, h)
    for h in (0, 1):
        for s, halves in ((5, (1, 0)), (6, (0, 1))):
            for chunk in range(per * halves[h], per * halves[h] + per):
                got(s, chunk)
            to_core(s, halves[h])
            tile(s, halves[h])
        got_core(9, h)
        tile(9, h)
    for h in (0, 1):
        for s, halves in ((10, (1, 0)), (11, (0, 1))):
            got_core(s, halves[h])
            tile(s, halves[h])

    degree = jnp.sum(deg[...], axis=0, keepdims=True)
    root = lax.rsqrt(degree)
    irb[0] = root

    def to_partners(buf, send, recv):
        place = buf.at[0]
        remote(place, buf.at[1], send, recv, other).start()
        for dc in (0, 1):
            for slot, dy in ((3, 1), (2, -1), (4, 2)):
                remote(place, buf.at[slot + 5 * dc], send, recv, near(dc, dy, 0)).start()
            for slot, dy in ((6, 1), (5, -1)):
                remote(place, buf.at[slot + 5 * dc], send, recv, near(dc, dy, -step)).start()

    others = pl.ds(1, PARTNERS - 1)
    to_partners(irb, ir_sem.at[0], ir_sem.at[1])

    for slot in range(1, PARTNERS):
        st[:, pl.ds(slot * ROWS, ROWS)] = image(slot)
    unused, inverse = factorise(unpack(sum_end(0, 8)))
    st[...] = mm(inverse, st[...])
    q0 = st[:, pl.ds(0, ROWS)]
    out_ref[pl.ds(0, BLOCK), :] = q0

    arrived(irb.at[others], ir_sem.at[1])
    for slot in range(PARTNERS):
        high, low = split(st[:, pl.ds(slot * ROWS, ROWS)] * irb[slot])
        zb[slot, pl.ds(0, BLOCK), :] = high
        zb[slot, pl.ds(BLOCK, BLOCK), :] = low

    def apply(buf):
        total = jnp.zeros((2 * BLOCK, ROWS), F32)
        rest = jnp.zeros((BLOCK, ROWS), F32)
        for slot in range(PARTNERS):
            vectors = buf[slot]
            total = total + jnp.dot(vectors, kh[slot], preferred_element_type=F32)
            rest = rest + jnp.dot(vectors[:BLOCK, :], kl[slot], preferred_element_type=F32)
        return (total[:BLOCK, :] + (total[BLOCK:, :] + rest)) * irb[0]

    w0 = apply(zb)
    u0 = w0 - q0
    high, low = split(u0 * irb[0])
    vb[0, pl.ds(0, BLOCK), :] = high
    vb[0, pl.ds(BLOCK, BLOCK), :] = low
    moments = mm_t(jnp.concatenate([q0, u0], axis=0), u0)
    sum_start(1, jnp.concatenate([pack(moments[:BLOCK, :]), pack(moments[BLOCK:, :])], axis=0))
    to_partners(vb, v_sem.at[0], v_sem.at[1])
    sum_plane(1, 16)
    sum_line(1, 16)
    arrived(vb.at[others], v_sem.at[1])
    v2 = apply(vb)

    def eye():
        shape = (BLOCK, BLOCK)
        same = lax.broadcasted_iota(jnp.int32, shape, 0) == lax.broadcasted_iota(jnp.int32, shape, 1)
        return jnp.where(same, 1.0, 0.0).astype(F32)

    summed = sum_end(1, 16)
    e0 = unpack(summed[:8, :])
    e0_t = e0.T
    coef_ref[0] = e0 + eye()
    b0, inverse = factorise(unpack(summed[8:, :]) - mm(e0_t, e0))
    coef_ref[1] = b0
    pair = jnp.concatenate([u0, v2], axis=1) - mm(e0_t, jnp.concatenate([q0, w0], axis=1))
    pair = mm(inverse, pair)
    q1 = pair[:, :ROWS]
    out_ref[pl.ds(BLOCK, BLOCK), :] = q1
    u1 = pair[:, ROWS:] - mm(b0, q0) - q1
    moments = mm_t(jnp.concatenate([q1, u1], axis=0), u1)
    sum_start(2, jnp.concatenate([pack(moments[:BLOCK, :]), pack(moments[BLOCK:, :])], axis=0))
    sum_plane(2, 16)
    sum_line(2, 16)

    arrived(xb.at[pl.ds(0, PARTNERS - 1)], x_send)
    arrived(irb.at[others], ir_sem.at[0])
    arrived(vb.at[others], v_sem.at[0])
    sum_drain(0, 8)
    sum_drain(1, 16)

    summed = sum_end(2, 16)
    e1 = unpack(summed[:8, :])
    e1_t = e1.T
    coef_ref[2] = e1 + eye()
    b1, inverse = factorise(unpack(summed[8:, :]) - mm(e1_t, e1))
    coef_ref[3] = b1
    out_ref[pl.ds(2 * BLOCK, BLOCK), :] = mm(inverse, u1 - mm(e1_t, q1))
    sum_drain(2, 16)


def local(snapshots, bins, pairs, start_weights):
    rows, features = snapshots.shape
    vmem = pl.BlockSpec(memory_space=pltpu.VMEM)
    basis, coefficients = pl.pallas_call(
        kernel,
        out_shape=(
            jax.ShapeDtypeStruct((3 * BLOCK, rows), F32),
            jax.ShapeDtypeStruct((4, BLOCK, BLOCK), F32),
        ),
        in_specs=[vmem] * 4,
        out_specs=(vmem, vmem),
        scratch_shapes=[
            pltpu.VMEM((PARTNERS, rows, features), BF16),
            pltpu.VMEM((PARTNERS, rows, rows), BF16),
            pltpu.VMEM((PARTNERS, rows, rows), BF16),
            pltpu.VMEM((PARTNERS, rows, WINDOW), BF16),
            pltpu.VMEM((WINDOW, rows), BF16),
            pltpu.VMEM((BLOCK, PARTNERS * rows), F32),
            pltpu.VMEM((8, rows), F32),
            pltpu.VMEM((8, rows), F32),
            pltpu.VMEM((PARTNERS, 1, rows), F32),
            pltpu.VMEM((PARTNERS, 2 * BLOCK, rows), BF16),
            pltpu.VMEM((PARTNERS, 2 * BLOCK, rows), BF16),
            pltpu.VMEM((3, 2, 16, 128), F32),
            pltpu.VMEM((3, NX * NY, 16, 128), F32),
            pltpu.VMEM((3, NZ, 16, 128), F32),
            pltpu.SemaphoreType.DMA,
            pltpu.SemaphoreType.DMA((5, CHUNKS)),
            pltpu.SemaphoreType.DMA((5, 2)),
            pltpu.SemaphoreType.DMA((1, 1)),
            pltpu.SemaphoreType.DMA((2,)),
            pltpu.SemaphoreType.DMA((2,)),
            pltpu.SemaphoreType.DMA((3, 6)),
        ],
        compiler_params=pltpu.CompilerParams(
            collective_id=0, has_side_effects=True, vmem_limit_bytes=48 << 20
        ),
    )(snapshots, bins.reshape(-1, 128), pairs.T, start_weights.T)
    return basis.T, coefficients


def solution(mesh):
    in_specs = (P(("loop", "inner"), None), P(), P(), P())
    out_specs = (P(("loop", "inner"), None), P())
    return jax.shard_map(local, mesh=mesh, in_specs=in_specs, out_specs=out_specs, check_vma=False)
```

time: 581 us -> 86.5 us (0.15)
  blocking collectives: 413 us -> 0 us
  waiting for transfers between devices: 85.5 us -> 0 us
  Pallas kernels: 0 us -> 80.8 us
  other arithmetic: 26.3 us -> 0 us
  matrix products: 18.7 us -> 0 us
  starting transfers between devices: 17.9 us -> 0 us
  between operations: 14.3 us -> 0.65 us
    psum x5 -> x0, blocking collectives: 398 us -> none  [the longest x2 157 us: local(): projected = lax.psum(local_gram(current, image), ('loop', 'inner'))]
    ppermute x6 -> x0, waiting for transfers between devices: 84.8 us -> none  [the longest x3 50.5 us: extended(): lax.ppermute(tail, axis, [(i, (i + 1) % count) for i in range(ends)])]
    pallas_call x0 -> x1, Pallas kernels: none -> 80.8 us  [local(): pl.pallas_call(kernel, out_shape=(jax.ShapeDtypeStruct((3 * BLOCK, rows),...]
    another operation x16 -> x0, other arithmetic: 20.6 us -> none  [the longest x9 10.8 us: finish(): lower_factor = jnp.linalg.cholesky(gram_total)]
    dot_general x15 -> x0, matrix products: 18 us -> none  [the longest x2 6.25 us: local(): total = jnp.dot(current_kernel(0), strip, precision=lax.Precision.HIGHEST)]
    ppermute x6 -> x0, starting transfers between devices: 17.9 us -> none  [the longest x3 14 us: extended(): lax.ppermute(tail, axis, [(i, (i + 1) % count) for i in range(ends)])]
    all_gather x2 -> x0, blocking collectives: 14.7 us -> none  [local(): vec_stack = lax.all_gather(scaled[None], 'loop', axis=0, tiled=True)]
  transfers between devices with their start and end apart: 7 -> 0, of which waited for: 6 -> 0; matrix products, arithmetic and copies ran while one was open for 2% -> 0% of each run, Pallas kernels for 0% -> 0%
where the time goes in v1:
time: 86.5 us; the launch traced here: 86.3 us
  Pallas kernels  80.8 us (93%)
  local copies, waits for them, and re-layouts  4.81 us (6%)
    pallas_call x1, Pallas kernels, local(): pl.pallas_call(kernel, out_shape=(jax.ShapeDtypeStruct((3 * BLOCK, rows),...  80.8 us
    unnamed x10, local copies, waits for them, and re-layouts  4.81 us

profile of v1, /device:TPU:1, one launch (start us, length us, event | category | flops | bytes accessed | tf_op | source)
XLA Modules:
  0.0 86.3 jit_solution(13120491186138350477)
XLA Ops:
  0.6 0.0 copy-start
  0.6 1.0 %copy-done = bf16[256,1024]{1,0:T(8,128)(2,1)S(1)} copy-done((bf16[256,1024]{1,0:T(8,128)(2,1)S(1)}, bf16[256,1024]{1,0:T(8,128)(2,1)}, u32[]{:S(2)}) %copy-start) | copy-done | bytes 524312
  1.7 0.0 copy-start.1
  1.7 0.9 %copy-done.1 = s32[65536]{0:T(1024)S(1)} copy-done((s32[65536]{0:T(1024)S(1)}, s32[65536]{0:T(1024)}, u32[]{:S(2)}) %copy-start.1) | copy-done | bytes 262168
  2.6 0.0 copy-start.2
  2.6 0.8 copy-done.2
  3.5 0.0 copy-start.3
  3.5 0.7 copy-done.3
  4.2 80.8 %shard_map.59 = (f32[96,256]{1,0:T(8,128)S(1)}, f32[4,32,32]{2,1,0:T(8,128)S(1)}) custom-call(bf16[256,1024]{1,0:T(8,128)(2,1)S(1)} %copy-done, s32[512,128]{1,0:T(8,128)S(1)} %bitcast.4, s32[2,2048]{1,0:T(2,128)S(1)} %bitcast.7, bf16[32,1024]{1,0:T(8,128)(2,1)S(1)} %bitcast.6), custom_call_target="tpu_custom_call" | custom-call | tf_op jit(solution)/shard_map/pallas_call | solution.py:407
  85.0 0.6 copy.8
  85.6 0.6 copy.9
Async XLA Ops:
  0.6 1.0 %copy-start = (bf16[256,1024]{1,0:T(8,128)(2,1)S(1)}, bf16[256,1024]{1,0:T(8,128)(2,1)}, u32[]{:S(2)}) copy-start(bf16[256,1024]{1,0:T(8,128)(2,1)} %x_ref.1) | copy-start | bytes 1572868
  1.7 0.9 %copy-start.1 = (s32[65536]{0:T(1024)S(1)}, s32[65536]{0:T(1024)}, u32[]{:S(2)}) copy-start(s32[65536]{0:T(1024)} %param.5) | copy-start | bytes 786436
  2.6 0.8 copy-start.2
  3.5 0.7 copy-start.3

commit v2 on v1

--- a/solution.py
+++ b/solution.py
@@ -18,9 +18,9 @@
 ROWS = 256
 BLOCK = 32
 PARTNERS = 12
-CHUNKS = 4
+CHUNKS = 8
 CHUNK = ROWS // CHUNKS
-DIRECT = 1
+DIRECT = 3
 HALF = ROWS // 2
 
 
@@ -56,23 +56,39 @@
     work = jnp.concatenate([gram, eye], axis=1)
     below = lax.broadcasted_iota(jnp.int32, (BLOCK, 2 * BLOCK), 0)
     scale = jnp.zeros((BLOCK, 2 * BLOCK), F32)
-    for k in range(BLOCK):
-        row = jnp.broadcast_to(work[k : k + 1, :], (BLOCK, 2 * BLOCK))
-        column = jnp.broadcast_to(work[:, k : k + 1], (BLOCK, 2 * BLOCK))
-        pivot = jnp.broadcast_to(column[k : k + 1, :], (BLOCK, 2 * BLOCK))
-        scale = jnp.where(below == k, pivot, scale)
-        work = work - jnp.where(below > k, column / pivot, 0.0) * row
+    for k in range(0, BLOCK, 2):
+        first = jnp.broadcast_to(work[:, k : k + 1], (BLOCK, 2 * BLOCK))
+        second = jnp.broadcast_to(work[:, k + 1 : k + 2], (BLOCK, 2 * BLOCK))
+        row, next_row = work[k : k + 1, :], work[k + 1 : k + 2, :]
+        pivot, cross = first[k : k + 1, :], second[k : k + 1, :]
+        inverse = 1.0 / pivot
+        ratio = first[k + 1 : k + 2, :] * inverse
+        next_row = next_row - ratio * row
+        next_pivot = second[k + 1 : k + 2, :] - ratio * cross
+        second = second - first * (cross * inverse)
+        change = first * (row * inverse) + second * (next_row * (1.0 / next_pivot))
+        scale = jnp.where(below == k, pivot, jnp.where(below == k + 1, next_pivot, scale))
+        work = jnp.where(below == k + 1, next_row, work) - jnp.where(below > k + 1, change, 0.0)
     work = work * lax.rsqrt(scale)
     upper = jnp.where(lane >= sub, work[:, :BLOCK], 0.0)
     return upper, work[:, BLOCK:]
 
 
 def kernel(
-    x_ref, bins_ref, pairs_ref, wt_ref, out_ref, coef_ref,
-    xb, kh, kl, hot, links, st, sq_row, deg, irb, zb, vb, core_buf, plane_buf, line_buf,
-    x_send, x_first, x_fwd, x_core, ir_sem, v_sem, ar_sem,
+    x_hbm, bins_hbm, pairs_hbm, wt_hbm, out_ref, coef_ref,
+    bins_ref, pairs_ref, wt_ref, xb, kh, kl, hot, links, st, sq_row, deg, irb, zb, vb, core_buf, plane_buf, line_buf,
+    x_send, x_first, x_fwd, x_core, ir_sem, v_sem, ar_sem, in_sem,
 ):
-    features = x_ref.shape[1]
+    x_ref = xb.at[0]
+    arrivals = [
+        pltpu.make_async_copy(src, dst, in_sem.at[n])
+        for n, (src, dst) in enumerate(
+            ((x_hbm, x_ref), (wt_hbm, wt_ref), (pairs_hbm, pairs_ref), (bins_hbm, bins_ref))
+        )
+    ]
+    for copy in arrivals:
+        copy.start()
+    features = xb.shape[2]
     group = lax.axis_index("loop")
     inner = lax.axis_index("inner")
     core = group % 2
@@ -102,6 +118,7 @@
     for d in greeted:
         pl.semaphore_signal(barrier, inc=1, device_id=d, device_id_type=MESH)
     pl.semaphore_wait(barrier, len(greeted))
+    arrivals[0].wait()
 
     def remote(src, dst, send, recv, target):
         return pltpu.make_async_remote_copy(
@@ -174,10 +191,12 @@
         arrived(plane_buf.at[n, pl.ds(0, NX * NY - 1), pl.ds(0, rows)], ar_sem.at[n, 2])
         arrived(line_buf.at[n, pl.ds(0, NZ - 1), pl.ds(0, rows)], ar_sem.at[n, 4])
 
+    for copy in arrivals[1:]:
+        copy.wait()
+
     own = x_ref[...]
     wt = wt_ref[...]
     start = lax.dot_general(wt, own, (((1,), (1,)), ((), ())), preferred_element_type=F32)
-    st[:, pl.ds(0, ROWS)] = start
     sum_start(0, pack(mm_t(start, start)))
 
     pairs = pairs_ref[...]
@@ -230,7 +249,6 @@
     norms = lax.dot_general(ones, sq_high, (((1,), (1,)), ((), ())), preferred_element_type=F32)
     norms = norms + lax.dot_general(ones, sq_low, (((1,), (1,)), ((), ())), preferred_element_type=F32)
     sq_row[...] = norms[0:8, :]
-    xb[0] = own
     deg[...] = jnp.zeros_like(deg)
 
     def tile(slot, half):
@@ -246,13 +264,13 @@
         high, low = split(value)
         kh[slot, span, :] = high
         kl[slot, span, :] = low
+        st[:, pl.ds(slot * ROWS + half * HALF, HALF)] = lax.dot_general(
+            wt_ref[...], theirs, (((1,), (1,)), ((), ())), preferred_element_type=F32
+        )
 
     def whole(slot):
         tile(slot, 0)
         tile(slot, 1)
-
-    def image(slot):
-        return lax.dot_general(wt_ref[...], xb[slot], (((1,), (1,)), ((), ())), preferred_element_type=F32)
 
     def forward(slot, chunk, target_slot, recv, target):
         push(slot, target_slot, chunk, recv, target)
@@ -329,8 +347,6 @@
     others = pl.ds(1, PARTNERS - 1)
     to_partners(irb, ir_sem.at[0], ir_sem.at[1])
 
-    for slot in range(1, PARTNERS):
-        st[:, pl.ds(slot * ROWS, ROWS)] = image(slot)
     unused, inverse = factorise(unpack(sum_end(0, 8)))
     st[...] = mm(inverse, st[...])
     q0 = st[:, pl.ds(0, ROWS)]
@@ -410,9 +426,12 @@
             jax.ShapeDtypeStruct((3 * BLOCK, rows), F32),
             jax.ShapeDtypeStruct((4, BLOCK, BLOCK), F32),
         ),
-        in_specs=[vmem] * 4,
+        in_specs=[pl.BlockSpec(memory_space=pl.ANY)] * 4,
         out_specs=(vmem, vmem),
         scratch_shapes=[
+            pltpu.VMEM((bins.shape[0] // 128, 128), jnp.int32),
+            pltpu.VMEM((2, pairs.shape[0]), jnp.int32),
+            pltpu.VMEM(start_weights.shape[::-1], BF16),
             pltpu.VMEM((PARTNERS, rows, features), BF16),
             pltpu.VMEM((PARTNERS, rows, rows), BF16),
             pltpu.VMEM((PARTNERS, rows, rows), BF16),
@@ -434,9 +453,10 @@
             pltpu.SemaphoreType.DMA((2,)),
             pltpu.SemaphoreType.DMA((2,)),
             pltpu.SemaphoreType.DMA((3, 6)),
+            pltpu.SemaphoreType.DMA((4,)),
         ],
         compiler_params=pltpu.CompilerParams(
-            collective_id=0, has_side_effects=True, vmem_limit_bytes=48 << 20
+            collective_id=0, has_side_effects=True, vmem_limit_bytes=62 << 20
         ),
     )(snapshots, bins.reshape(-1, 128), pairs.T, start_weights.T)
     return basis.T, coefficients

time: 86.5 us -> 77.4 us (0.89)
  Pallas kernels: 80.8 us -> 74.4 us
  local copies, waits for them, and re-layouts: 4.81 us -> 2.2 us
    pallas_call x1, Pallas kernels: 80.8 us -> 74.4 us  [local(): pl.pallas_call(kernel, out_shape=(jax.ShapeDtypeStruct((3 * BLOCK, rows),...]
    unnamed x10 -> x4, local copies, waits for them, and re-layouts: 4.81 us -> 2.2 us
where the time goes in v2:
time: 77.4 us; the launch traced here: 77.3 us
  Pallas kernels  74.4 us (96%)
  local copies, waits for them, and re-layouts  2.2 us (3%)
    pallas_call x1, Pallas kernels, local(): pl.pallas_call(kernel, out_shape=(jax.ShapeDtypeStruct((3 * BLOCK, rows),...  74.4 us
    unnamed x4, local copies, waits for them, and re-layouts  2.2 us

profile of v2, /device:TPU:1, one launch (start us, length us, event | category | flops | bytes accessed | tf_op | source)
XLA Modules:
  0.0 77.3 jit_solution(14167804111855857699)
XLA Ops:
  0.6 74.4 %shard_map.59 = (f32[96,256]{1,0:T(8,128)}, f32[4,32,32]{2,1,0:T(8,128)}) custom-call(bf16[256,1024]{1,0:T(8,128)(2,1)} %x_hbm.1, s32[512,128]{1,0:T(8,128)} %bitcast.4, s32[2,2048]{1,0:T(2,128)} %bitcast.7, bf16[32,1024]{1,0:T(8,128)(2,1)} %bitcast.6), custom_call_target="tpu_custom_call" | custom-call | tf_op jit(solution)/shard_map/pallas_call | solution.py:423
  75.0 0.0 copy-start
  75.0 1.6 %copy.8 = f32[256,96]{0,1:T(8,128)} copy(f32[256,96]{0,1:T(8,128)} %bitcast.5) | data formatting | bytes 196608
  76.6 0.0 copy-done
  76.6 0.6 copy.9
Async XLA Ops:
  75.0 1.6 %copy-start = (f32[4,32,32]{2,1,0:T(8,128)S(1)}, f32[4,32,32]{2,1,0:T(8,128)}, u32[]{:S(2)}) copy-start(f32[4,32,32]{2,1,0:T(8,128)} %get-tuple-element.9) | copy-start | bytes 49156

commit v3 on v2

--- a/solution.py
+++ b/solution.py
@@ -77,7 +77,7 @@
 def kernel(
     x_hbm, bins_hbm, pairs_hbm, wt_hbm, out_ref, coef_ref,
     bins_ref, pairs_ref, wt_ref, xb, kh, kl, hot, links, st, sq_row, deg, irb, zb, vb, core_buf, plane_buf, line_buf,
-    x_send, x_first, x_fwd, x_core, ir_sem, v_sem, ar_sem, in_sem,
+    x_send, x_first, x_fwd, x_core, ir_sem, v_sem, ar_sem, in_sem, root_sem,
 ):
     x_ref = xb.at[0]
     arrivals = [
@@ -337,48 +337,56 @@
 
     def to_partners(buf, send, recv):
         place = buf.at[0]
-        remote(place, buf.at[1], send, recv, other).start()
-        for dc in (0, 1):
-            for slot, dy in ((3, 1), (2, -1), (4, 2)):
-                remote(place, buf.at[slot + 5 * dc], send, recv, near(dc, dy, 0)).start()
+
+        def to(slot, target):
+            remote(place, buf.at[slot], send, recv(slot), target).start()
+
+        for dc in (1, 0):
             for slot, dy in ((6, 1), (5, -1)):
-                remote(place, buf.at[slot + 5 * dc], send, recv, near(dc, dy, -step)).start()
+                to(slot + 5 * dc, near(dc, dy, -step))
+        for dc in (1, 0):
+            for slot, dy in ((4, 2), (3, 1), (2, -1)):
+                to(slot + 5 * dc, near(dc, dy, 0))
+        to(1, other)
 
     others = pl.ds(1, PARTNERS - 1)
-    to_partners(irb, ir_sem.at[0], ir_sem.at[1])
+    to_partners(irb, ir_sem.at[0], lambda slot: root_sem.at[slot])
 
     unused, inverse = factorise(unpack(sum_end(0, 8)))
     st[...] = mm(inverse, st[...])
     q0 = st[:, pl.ds(0, ROWS)]
     out_ref[pl.ds(0, BLOCK), :] = q0
 
-    arrived(irb.at[others], ir_sem.at[1])
-    for slot in range(PARTNERS):
-        high, low = split(st[:, pl.ds(slot * ROWS, ROWS)] * irb[slot])
-        zb[slot, pl.ds(0, BLOCK), :] = high
-        zb[slot, pl.ds(BLOCK, BLOCK), :] = low
-
-    def apply(buf):
+
+    def apply(buf, arrive):
         total = jnp.zeros((2 * BLOCK, ROWS), F32)
         rest = jnp.zeros((BLOCK, ROWS), F32)
-        for slot in range(PARTNERS):
+        for slot in (0, 1, 2, 3, 7, 8, 4, 9, 5, 6, 10, 11):
+            arrive(slot)
             vectors = buf[slot]
             total = total + jnp.dot(vectors, kh[slot], preferred_element_type=F32)
             rest = rest + jnp.dot(vectors[:BLOCK, :], kl[slot], preferred_element_type=F32)
         return (total[:BLOCK, :] + (total[BLOCK:, :] + rest)) * irb[0]
 
-    w0 = apply(zb)
+    def scale_start(slot):
+        if slot > 0:
+            arrived(irb.at[slot], root_sem.at[slot])
+        high, low = split(st[:, pl.ds(slot * ROWS, ROWS)] * irb[slot])
+        zb[slot, pl.ds(0, BLOCK), :] = high
+        zb[slot, pl.ds(BLOCK, BLOCK), :] = low
+
+    w0 = apply(zb, scale_start)
     u0 = w0 - q0
     high, low = split(u0 * irb[0])
     vb[0, pl.ds(0, BLOCK), :] = high
     vb[0, pl.ds(BLOCK, BLOCK), :] = low
     moments = mm_t(jnp.concatenate([q0, u0], axis=0), u0)
     sum_start(1, jnp.concatenate([pack(moments[:BLOCK, :]), pack(moments[BLOCK:, :])], axis=0))
-    to_partners(vb, v_sem.at[0], v_sem.at[1])
+    to_partners(vb, v_sem.at[0], lambda slot: v_sem.at[1])
     sum_plane(1, 16)
     sum_line(1, 16)
     arrived(vb.at[others], v_sem.at[1])
-    v2 = apply(vb)
+    v2 = apply(vb, lambda slot: None)
 
     def eye():
         shape = (BLOCK, BLOCK)
@@ -454,6 +462,7 @@
             pltpu.SemaphoreType.DMA((2,)),
             pltpu.SemaphoreType.DMA((3, 6)),
             pltpu.SemaphoreType.DMA((4,)),
+            pltpu.SemaphoreType.DMA((PARTNERS,)),
         ],
         compiler_params=pltpu.CompilerParams(
             collective_id=0, has_side_effects=True, vmem_limit_bytes=62 << 20

time: 77.4 us -> 76.5 us (0.988)
  Pallas kernels: 74.4 us -> 73.5 us
    pallas_call x1, Pallas kernels: 74.4 us -> 73.5 us  [local(): pl.pallas_call(kernel, out_shape=(jax.ShapeDtypeStruct((3 * BLOCK, rows),...]
where the time goes in v3:
time: 76.5 us; the launch traced here: 76.4 us
  Pallas kernels  73.5 us (96%)
  local copies, waits for them, and re-layouts  2.2 us (3%)
    pallas_call x1, Pallas kernels, local(): pl.pallas_call(kernel, out_shape=(jax.ShapeDtypeStruct((3 * BLOCK, rows),...  73.5 us
    unnamed x4, local copies, waits for them, and re-layouts  2.2 us

profile of v3, /device:TPU:1, one launch (start us, length us, event | category | flops | bytes accessed | tf_op | source)
XLA Modules:
  0.0 76.4 jit_solution(8815078382300651423)
XLA Ops:
  0.6 73.5 %shard_map.59 = (f32[96,256]{1,0:T(8,128)}, f32[4,32,32]{2,1,0:T(8,128)}) custom-call(bf16[256,1024]{1,0:T(8,128)(2,1)} %x_hbm.1, s32[512,128]{1,0:T(8,128)} %bitcast.4, s32[2,2048]{1,0:T(2,128)} %bitcast.7, bf16[32,1024]{1,0:T(8,128)(2,1)} %bitcast.6), custom_call_target="tpu_custom_call" | custom-call | tf_op jit(solution)/shard_map/pallas_call | solution.py:431
  74.2 0.0 copy-start
  74.2 1.6 %copy.8 = f32[256,96]{0,1:T(8,128)} copy(f32[256,96]{0,1:T(8,128)} %bitcast.5) | data formatting | bytes 196608
  75.7 0.0 copy-done
  75.7 0.6 copy.9
Async XLA Ops:
  74.2 1.6 %copy-start = (f32[4,32,32]{2,1,0:T(8,128)S(1)}, f32[4,32,32]{2,1,0:T(8,128)}, u32[]{:S(2)}) copy-start(f32[4,32,32]{2,1,0:T(8,128)} %get-tuple-element.9) | copy-start | bytes 49156
